TPU v7x, 128 devices: a whole 4x4x4 slice. The times are simulated.
128 devices in a mesh: dp: 4 (over z_lo, core), seq: 32 (over x, z_hi, y).
Axes of the slice: x: 4, y: 4, z: 4 (z_hi: 2, z_lo: 2; z = z_hi * 2 + z_lo), core: 2. Of those that a mesh axis runs over, the one named last changes fastest.
Arguments:
- latents: bfloat16 [4, 16, 512, 1152], P('dp', None, 'seq'), may hold values from -40 to 40
- shift_mod: bfloat16 [4, 1152], P('dp'), may hold values from -2.5 to 2.5
- scale_mod: bfloat16 [4, 1152], P('dp'), may hold values from -2.5 to 2.5
- gate_mod: bfloat16 [4, 1152], P('dp'), may hold values from 0.5 to 1.5
- qkv_weight: bfloat16 [1152, 3456], replicated, may hold values from -16 to 16
- out_weight: bfloat16 [1152, 1152], replicated, may hold values from -0.1875 to 0.1875
- cotangent: bfloat16 [4, 16, 512, 1152], P('dp', None, 'seq'), may hold values from -6 to 6
Outputs:
- block_out: bfloat16 [4, 16, 512, 1152], P('dp', None, 'seq')
- latent_grad: bfloat16 [4, 16, 512, 1152], P('dp', None, 'seq')
- qkv_weight_grad: float32 [1152, 3456], P(('dp', 'seq'))
- out_weight_grad: float32 [1152, 1152], P(('dp', 'seq'))
All inputs are finite; a program needn't handle non-finite values.
Results may differ from a plain program's by a relative error of at most 0.022.
The roundings to bfloat16 on the way count: a program that leaves them out, or rounds other values in their place, can miss the bound.
Values may be sent and summed in bfloat16 or wider, within the bound.
A program may use at most 128 MiB of HBM per device.

v0:
```python
import math

import jax
import jax.numpy as jnp
from jax import lax
from jax.sharding import PartitionSpec as P

H = 16
HG = 2


EPS = 1e-06


def norm_rows(values):
    floats = values.astype(jnp.float32)
    centre = jnp.mean(floats, -1, keepdims=True)
    shifted = floats - centre
    variance = jnp.mean(shifted * shifted, -1, keepdims=True)
    inverse = lax.rsqrt(variance + EPS)
    return (shifted * inverse, inverse)


def contract(left, right):
    return lax.dot_general(
        left, right, (((0,), (0,)), ((), ())), preferred_element_type=jnp.float32
    )


def split_items(values, frames, groups, devices):
    local = values.shape[0] // frames
    inner = values.shape[1] // (groups * HG)
    shaped = values.reshape(frames, local, groups, HG, inner).transpose(3, 0, 1, 2, 4)
    return shaped.reshape(devices, HG * frames // devices, local, groups * inner)


def merge_items(items, frames, groups):
    local = items.shape[2]
    inner = items.shape[3] // groups
    shaped = items.reshape(HG, frames, local, groups, inner).transpose(1, 2, 3, 0, 4)
    return shaped.reshape(frames * local, groups * HG * inner)


def attend_item(projected, heads, size):
    length = projected.shape[0]
    parts = projected.reshape(length, 3, heads, size)
    query, keys, values = (parts[:, 0], parts[:, 1], parts[:, 2])
    block = min(512, length)
    query_blocks = query.reshape(length // block, block, heads, size)

    def one_block(query_block):
        scores = jnp.einsum(
            "qhd,khd->hqk", query_block, keys, preferred_element_type=jnp.float32
        ) / math.sqrt(size)
        probs = jax.nn.softmax(scores, -1).astype(jnp.bfloat16)
        mixed = jnp.einsum("hqk,khd->qhd", probs, values, preferred_element_type=jnp.float32)
        return mixed.astype(jnp.bfloat16)

    return lax.map(one_block, query_blocks).reshape(length, heads * size)


def attend_back(projected, upstream, heads, size):
    length = projected.shape[0]
    parts = projected.reshape(length, 3, heads, size)
    query, keys, values = (parts[:, 0], parts[:, 1], parts[:, 2])
    block = min(512, length)
    query_blocks = query.reshape(length // block, block, heads, size)
    grad_blocks = upstream.reshape(length // block, block, heads, size)

    def one_block(carry, pair):
        key_acc, value_acc = carry
        query_block, grad_block = pair
        scores = jnp.einsum(
            "qhd,khd->hqk", query_block, keys, preferred_element_type=jnp.float32
        ) / math.sqrt(size)
        probs = jax.nn.softmax(scores, -1)
        value_acc = value_acc + jnp.einsum(
            "hqk,qhd->khd",
            probs.astype(jnp.bfloat16),
            grad_block,
            preferred_element_type=jnp.float32,
        )
        dprobs = jnp.einsum("qhd,khd->hqk", grad_block, values, preferred_element_type=jnp.float32)
        total = jnp.sum(probs * dprobs, -1, keepdims=True)
        score_grad = (probs * (dprobs - total) / math.sqrt(size)).astype(jnp.bfloat16)
        query_grad = jnp.einsum(
            "hqk,khd->qhd", score_grad, keys, preferred_element_type=jnp.float32
        ).astype(jnp.bfloat16)
        key_acc = key_acc + jnp.einsum(
            "hqk,qhd->khd", score_grad, query_block, preferred_element_type=jnp.float32
        )
        return ((key_acc, value_acc), query_grad)

    zeros = jnp.zeros((length, heads, size), jnp.float32)
    (key_grad, value_grad), query_grad = lax.scan(
        one_block, (zeros, zeros), (query_blocks, grad_blocks)
    )
    stacked = jnp.stack(
        [
            query_grad.reshape(length, heads, size),
            key_grad.astype(jnp.bfloat16),
            value_grad.astype(jnp.bfloat16),
        ],
        1,
    )
    return stacked.reshape(length, 3 * heads * size)


def on_device(latents, shift_mod, scale_mod, gate_mod, qkv_weight, out_weight, cotangent):
    devices = lax.axis_size("seq")
    frames = latents.shape[1]
    local = latents.shape[2]
    width = latents.shape[3]
    heads = H // HG
    size = width // H
    per_device = HG * frames // devices
    tokens = latents.reshape(frames * local, width)
    normed, inverse = norm_rows(tokens)
    lift = 1.0 + scale_mod.astype(jnp.float32)
    modulated = (normed * lift + shift_mod.astype(jnp.float32)).astype(jnp.bfloat16)
    spread = jnp.broadcast_to(
        modulated.reshape(frames, local, width)[None], (HG, frames, local, width)
    )
    spread = spread.reshape(devices, per_device, local, width)
    projected = jnp.dot(modulated, qkv_weight, preferred_element_type=jnp.float32).astype(
        jnp.bfloat16
    )
    blocks = lax.all_to_all(
        split_items(projected, frames, 3, devices), "seq", split_axis=0, concat_axis=2, tiled=True
    )
    mixed = lax.map(lambda item: attend_item(item, heads, size), blocks[0])
    heads_out = mixed[None]
    returned = lax.all_to_all(heads_out, "seq", split_axis=2, concat_axis=0, tiled=True)
    attended = merge_items(returned, frames, 1)
    gating = gate_mod.astype(jnp.float32)
    branch = jnp.dot(attended, out_weight, preferred_element_type=jnp.float32)
    block_out = (tokens.astype(jnp.float32) + gating * branch).astype(jnp.bfloat16)
    upstream = cotangent.reshape(frames * local, width).astype(jnp.float32)
    branch_grad = (gating * upstream).astype(jnp.bfloat16)
    attended_grad = lax.dot_general(
        branch_grad, out_weight, (((1,), (1,)), ((), ())), preferred_element_type=jnp.float32
    ).astype(jnp.bfloat16)
    out_weight_grad = lax.psum_scatter(
        contract(attended, branch_grad), ("dp", "seq"), scatter_dimension=0, tiled=True
    )
    grad_items = lax.all_to_all(
        split_items(attended_grad, frames, 1, devices),
        "seq",
        split_axis=0,
        concat_axis=2,
        tiled=True,
    )
    item_grads = lax.map(
        lambda pair: attend_back(pair[0], pair[1], heads, size), (blocks[0], grad_items[0])
    )
    sent_back = lax.all_to_all(item_grads[None], "seq", split_axis=2, concat_axis=0, tiled=True)
    projected_grad = merge_items(sent_back, frames, 3)
    modulated_grad = lax.dot_general(
        projected_grad, qkv_weight, (((1,), (1,)), ((), ())), preferred_element_type=jnp.float32
    )
    qkv_weight_grad = lax.psum_scatter(
        contract(modulated, projected_grad), ("dp", "seq"), scatter_dimension=0, tiled=True
    )
    normed_grad = modulated_grad * lift
    first = jnp.mean(normed_grad, -1, keepdims=True)
    second = jnp.mean(normed_grad * normed, -1, keepdims=True)
    latent_grad = (upstream + inverse * (normed_grad - first - normed * second)).astype(
        jnp.bfloat16
    )
    return (
        block_out.reshape(latents.shape),
        latent_grad.reshape(latents.shape),
        qkv_weight_grad,
        out_weight_grad,
    )


def solution(mesh):
    in_specs = (
        P("dp", None, "seq", None),
        P("dp", None),
        P("dp", None),
        P("dp", None),
        P(),
        P(),
        P("dp", None, "seq", None),
    )
    out_specs = (
        P("dp", None, "seq", None),
        P("dp", None, "seq", None),
        P(("dp", "seq"), None),
        P(("dp", "seq"), None),
    )
    return jax.shard_map(
        on_device, mesh=mesh, in_specs=in_specs, out_specs=out_specs, check_vma=False
    )
```

profile of v0, /device:TPU:1, one launch (start us, length us, event | category | flops | bytes accessed | tf_op | source)
XLA Modules:
  0.0 526.2 jit_solution(5943802690889254981)
XLA Ops:
  9.2 1.8 convolution_convert_fusion.1
  11.1 2.9 reshape.170
  14.0 2.0 copy.38
  16.0 11.3 %all-to-all-start.2 = ((bf16[32,1,16,576]{3,2,1,0:T(8,128)(2,1)}), bf16[32,1,16,576]{3,2,1,0:T(8,128)(2,1)}, u32[]{:S(2)}, u32[]{:S(2)}) async-start(bf16[32,1,16,576]{3,2,1,0:T(8,128)(2,1)} %bitcast.117), calls=%async_computation.2 | async-start | bytes 1310720 | tf_op jit(solution)/shard_map/all_to_all | solution.py:146
  28.3 7.0 %convolution_convert_fusion = bf16[256,3456]{1,0:T(8,128)(2,1)} fusion(bf16[256,1152]{1,0:T(8,128)(2,1)S(1)} %add_convert_fusion.1, bf16[1152,3456]{1,0:T(8,128)(2,1)} %param.11), kind=kOutput, calls=%fused_computation.8 | convolution fusion | flops 2039316480 | bytes 10321920 | tf_op jit(solution)/shard_map/dot_general | solution.py:125
  35.3 5.4 %reshape.164 = bf16[16,16,3,2,576]{4,3,2,1,0:T(2,128)(2,1)} reshape(bf16[256,3456]{1,0:T(8,128)(2,1)} %convolution_convert_fusion) | data formatting | bytes 3538944 | tf_op jit(solution)/shard_map/reshape | solution.py:33
  40.7 4.4 copy.56
  45.2 6.2 %reshape.165 = bf16[32,1,16,1728]{3,2,0,1:T(8,128)(2,1)} reshape(bf16[2,16,16,3,576]{4,3,2,1,0:T(4,128)(2,1)} %bitcast.111) | data formatting | bytes 3538944 | tf_op jit(solution)/shard_map/reshape | solution.py:34
  51.4 9.5 %all-to-all-start = ((bf16[32,1,16,1728]{3,2,1,0:T(8,128)(2,1)}), bf16[32,1,16,1728]{3,2,1,0:T(8,128)(2,1)}, u32[]{:S(2)}, u32[]{:S(2)}) async-start(bf16[32,1,16,1728]{3,2,1,0:T(8,128)(2,1)} %bitcast.113), calls=%async_computation | async-start | bytes 3670016 | tf_op jit(solution)/shard_map/all_to_all | solution.py:128
  60.8 3.0 squeeze.44
  63.8 2.4 copy.40
  66.2 20.0 %all-to-all-done = bf16[32,1,16,1728]{3,2,1,0:T(8,128)(2,1)} async-done(((bf16[32,1,16,1728]{3,2,1,0:T(8,128)(2,1)}), bf16[32,1,16,1728]{3,2,1,0:T(8,128)(2,1)}, u32[]{:S(2)}, u32[]{:S(2)}) %all-to-all-start) | async-done | bytes 1769504 | tf_op jit(solution)/shard_map/all_to_all | solution.py:128
  86.2 6.4 %reshape.166 = bf16[512,3,8,72]{3,2,1,0:T(8,128)(2,1)} reshape(bf16[32,1,16,1728]{3,2,1,0:T(8,128)(2,1)} %all-to-all-done) | data formatting | bytes 3538944 | tf_op jit(solution)/shard_map/while/body/eval_jaxpr/reshape | solution.py:46
  92.5 3.6 fusion.70
  96.2 2.3 copy.52
  98.5 2.3 copy.54
  100.8 2.3 copy.53
  103.2 7.2 %fusion.71 = (f32[8,512]{1,0:T(8,128)S(1)}, f32[8,512,512]{1,2,0:T(8,128)}) fusion(bf16[512,1,8,72]{0,3,2,1:T(8,128)(2,1)} %copy.54, bf16[512,1,8,72]{0,3,2,1:T(8,128)(2,1)} %copy.53), kind=kOutput, calls=%fused_computation.71 | convolution fusion | flops 308281856 | bytes 9584640 | tf_op jit(solution)/shard_map/while/body/eval_jaxpr/while/body/eval_jaxpr/sub | solution.py:55
  110.4 5.3 %fusion.21 = bf16[8,72,512]{2,1,0:T(8,128)(2,1)} fusion(bf16[512,1,8,72]{0,3,2,1:T(8,128)(2,1)} %copy.52, f32[8,512,512]{1,2,0:T(8,128)} %get-tuple-element.85, f32[8,512]{1,0:T(8,128)S(1)} %get-tuple-element.84), kind=kOutput, calls=%fused_computation.24 | convolution fusion | flops 306479104 | bytes 9584640 | tf_op jit(solution)/shard_map/while/body/eval_jaxpr/while/body/eval_jaxpr/hqk,khd->qhd/dot_general | solution.py:56
  115.7 3.7 copy.36
  119.9 6.6 %reduce.10 = bf16[512,576]{1,0:T(8,128)(2,1)} reduce(bf16[512,1,1,576]{3,2,1,0:T(2,128)(2,1)} %bitcast.115, bf16[]{:T(256)} %broadcast.119), dimensions={1,2}, to_apply=%bitcast.81.reduce_sub_computation | reduce | bytes 1179650
  126.5 3.3 reshape.184
  129.8 6.8 %all-to-all-start.1 = ((bf16[32,2,4608]{2,1,0:T(2,128)(2,1)}), bf16[32,2,4608]{2,1,0:T(2,128)(2,1)}, u32[]{:S(2)}, u32[]{:S(2)}) async-start(bf16[32,2,4608]{2,1,0:T(2,128)(2,1)} %reshape.184), calls=%async_computation.1 | async-start | bytes 1179648 | tf_op jit(solution)/shard_map/all_to_all | solution.py:133
  136.6 5.9 %fusion.39 = bf16[512,1,8,72]{0,3,2,1:T(8,128)(2,1)} fusion(bf16[512,8,72]{0,2,1:T(8,128)(2,1)} %copy.40, f32[8,512,512]{1,2,0:T(8,128)} %get-tuple-element.85, f32[8,512]{1,0:T(8,128)S(1)} %get-tuple-element.84), kind=kOutput, calls=%fused_computation.30 | convolution fusion | flops 306479104 | bytes 9584640 | tf_op jit(solution)/shard_map/while/body/eval_jaxpr/while/body/eval_jaxpr/hqk,qhd->khd/dot_general | solution.py:77
  142.5 4.5 fusion.61
  147.0 14.5 %fusion.33 = bf16[512,1,8,72]{0,3,2,1:T(8,128)(2,1)} fusion(f32[8,512,512]{1,2,0:T(8,128)} %fusion.61, bf16[512,1,8,72]{0,3,2,1:T(8,128)(2,1)} %copy.53, f32[8,512,512]{1,2,0:T(8,128)} %get-tuple-element.85, f32[8,512]{1,0:T(8,128)S(1)} %get-tuple-element.84), kind=kOutput, calls=%fused_computation.28 | convolution fusion | flops 316969472 | bytes 17973248 | tf_op jit(solution)/shard_map/while/body/eval_jaxpr/while/body/eval_jaxpr/hqk,qhd->khd/dot_general | solution.py:89
  161.5 15.1 %fusion.36 = bf16[512,1,8,72]{0,3,2,1:T(8,128)(2,1)} fusion(f32[8,512,512]{1,2,0:T(8,128)} %fusion.61, bf16[512,1,8,72]{0,3,2,1:T(8,128)(2,1)} %copy.54, f32[8,512,512]{1,2,0:T(8,128)} %get-tuple-element.85, f32[8,512]{1,0:T(8,128)S(1)} %get-tuple-element.84), kind=kOutput, calls=%fused_computation.29 | convolution fusion | flops 316969472 | bytes 17973248 | tf_op jit(solution)/shard_map/while/body/eval_jaxpr/while/body/eval_jaxpr/hqk,khd->qhd/dot_general | solution.py:86
  176.6 2.8 pad_maximum_fusion
  179.4 8.8 %copy.45 = bf16[1,1,512,1728]{3,1,0,2:T(2,128)(2,1)} copy(bf16[1,1,512,1728]{2,3,1,0:T(8,128)(2,1)} %bitcast.114) | data formatting | bytes 3538944 | tf_op jit(solution)/shard_map/broadcast_in_dim | solution.py:156
  188.2 13.3 %reduce.11 = bf16[512,1728]{1,0:T(8,128)(2,1)} reduce(bf16[512,1,1,1728]{3,2,1,0:T(2,128)(2,1)} %bitcast.110, bf16[]{:T(256)} %broadcast.119), dimensions={1,2}, to_apply=%bitcast.83.reduce_sub_computation | reduce | bytes 3538946
  201.6 5.7 %reshape.186 = bf16[32,2,13824]{2,1,0:T(2,128)(2,1)} reshape(bf16[512,1728]{1,0:T(8,128)(2,1)} %reduce.11) | data formatting | bytes 3538944
  207.3 9.3 %all-to-all-start.3 = ((bf16[32,2,13824]{2,1,0:T(2,128)(2,1)}), bf16[32,2,13824]{2,1,0:T(2,128)(2,1)}, u32[]{:S(2)}, u32[]{:S(2)}) async-start(bf16[32,2,13824]{2,1,0:T(2,128)(2,1)} %reshape.186), calls=%async_computation.3 | async-start | bytes 3538944 | tf_op jit(solution)/shard_map/all_to_all | solution.py:156
  216.6 2.0 fusion.42
  219.7 5.1 reshape.185
  226.2 1.5 copy.37
  227.8 2.7 reshape.168
  230.4 4.5 fusion.81
  235.0 4.1 all-to-all-done.3
  239.1 10.8 %reshape.187 = bf16[512,1,1,1728]{3,2,1,0:T(2,128)(2,1)} reshape(bf16[32,2,13824]{2,1,0:T(2,128)(2,1)} %all-to-all-done.3) | data formatting | bytes 3538944
  249.9 13.2 %bitcast_reduce_fusion = bf16[512,1728]{1,0:T(8,128)(2,1)} fusion(bf16[512,1,1,1728]{3,2,1,0:T(2,128)(2,1)} %reshape.187), kind=kLoop, calls=%fused_computation.72 | loop fusion | bytes 3538944 | tf_op jit(solution)/shard_map/all_to_all | solution.py:156
  263.1 6.3 %reshape.173 = bf16[2,16,16,3,576]{4,3,2,1,0:T(4,128)(2,1)} reshape(bf16[512,1728]{1,0:T(8,128)(2,1)} %bitcast_reduce_fusion) | data formatting | bytes 3538944 | tf_op jit(solution)/shard_map/reshape | solution.py:40
  269.4 6.0 %copy.46 = bf16[16,16,3,2,576]{4,3,2,1,0:T(2,128)(2,1)} copy(bf16[16,16,3,2,576]{4,2,1,0,3:T(4,128)(2,1)} %bitcast.112) | data formatting | bytes 3538944 | tf_op jit(solution)/shard_map/transpose | solution.py:40
  275.4 5.2 reshape.174
  280.6 9.6 %fusion.80 = f32[1152,3456]{1,0:T(8,128)} fusion(bf16[256,1152]{1,0:T(8,128)(2,1)} %bitcast.119, bf16[256,3456]{1,0:T(8,128)(2,1)} %reshape.174), kind=kOutput, calls=%fused_computation.73 | convolution fusion | flops 2038431744 | bytes 18284544 | tf_op jit(solution)/shard_map/dot_general | solution.py:25
  290.3 3.0 fusion.16
  293.3 6.1 %fusion.69 = (f32[256]{0:T(256)S(1)}, f32[256]{0:T(256)S(1)}, f32[256,1152]{1,0:T(8,128)S(1)}) fusion(f32[256]{0:T(256)S(1)} %rsqrt.13, f32[256]{0:T(256)S(1)} %div.56, bf16[1,16,16,1152]{3,2,1,0:T(8,128)(2,1)S(1)} %copy-done.1, f32[1152]{0:T(1024)S(1)} %get-tuple-element.88, bf16[256,3456]{1,0:T(8,128)(2,1)S(1)} %copy-done.2, bf16[1152,3456]{1,0:T(8,128)(2,1)} %param.11), kind=kOutput, calls=%fused_computation.69 | convolution fusion | flops 2040495616 | bytes 11510272 | tf_op jit(solution)/shard_map/dot_general | solution.py:158
  300.7 215.2 %all-reduce.5.cloned.1.call-done = (f32[1152,3456]{1,0:T(8,128)}, f32[1152,1152]{1,0:T(8,128)}) async-done(((f32[1152,3456]{1,0:T(8,128)}, f32[1152,1152]{1,0:T(8,128)}), (f32[1152,3456]{1,0:T(8,128)}, f32[1152,1152]{1,0:T(8,128)})) %all-reduce.5.cloned.1.call-update) | async-done | bytes 21233680
  515.9 1.7 constant_dynamic-slice_fusion.1
  (37 shorter events, 9.0 us)
Async XLA Ops:
  7.2 2.0 copy-start
  11.1 16.2 %copy-start.1 = (bf16[1,16,16,1152]{3,2,1,0:T(8,128)(2,1)S(1)}, bf16[1,16,16,1152]{3,2,1,0:T(8,128)(2,1)}, u32[]{:S(2)}) copy-start(bf16[1,16,16,1152]{3,2,1,0:T(8,128)(2,1)} %param.7) | copy-start | bytes 1769476
  11.1 16.9 %copy-start.6 = (bf16[1,1152]{1,0:T(2,128)(2,1)S(1)}, bf16[1,1152]{1,0:T(2,128)(2,1)}, u32[]{:S(2)}) copy-start(bf16[1,1152]{1,0:T(2,128)(2,1)} %param.8) | copy-start | bytes 6916
  11.1 16.9 %copy-start.7 = (bf16[1,1152]{1,0:T(2,128)(2,1)S(1)}, bf16[1,1152]{1,0:T(2,128)(2,1)}, u32[]{:S(2)}) copy-start(bf16[1,1152]{1,0:T(2,128)(2,1)} %param.9) | copy-start | bytes 6916
  16.0 35.4 %all-to-all-start.2 = ((bf16[32,1,16,576]{3,2,1,0:T(8,128)(2,1)}), bf16[32,1,16,576]{3,2,1,0:T(8,128)(2,1)}, u32[]{:S(2)}, u32[]{:S(2)}) async-start(bf16[32,1,16,576]{3,2,1,0:T(8,128)(2,1)} %bitcast.117), calls=%async_computation.2 | async-start | bytes 1310720 | tf_op jit(solution)/shard_map/all_to_all | solution.py:146
  51.4 34.8 %all-to-all-start = ((bf16[32,1,16,1728]{3,2,1,0:T(8,128)(2,1)}), bf16[32,1,16,1728]{3,2,1,0:T(8,128)(2,1)}, u32[]{:S(2)}, u32[]{:S(2)}) async-start(bf16[32,1,16,1728]{3,2,1,0:T(8,128)(2,1)} %bitcast.113), calls=%async_computation | async-start | bytes 3670016 | tf_op jit(solution)/shard_map/all_to_all | solution.py:128
  129.8 77.5 %all-to-all-start.1 = ((bf16[32,2,4608]{2,1,0:T(2,128)(2,1)}), bf16[32,2,4608]{2,1,0:T(2,128)(2,1)}, u32[]{:S(2)}, u32[]{:S(2)}) async-start(bf16[32,2,4608]{2,1,0:T(2,128)(2,1)} %reshape.184), calls=%async_computation.1 | async-start | bytes 1179648 | tf_op jit(solution)/shard_map/all_to_all | solution.py:133
  136.6 5.9 %copy-start.4 = (bf16[512,8,72]{0,2,1:T(8,128)(2,1)S(1)}, bf16[512,8,72]{0,2,1:T(8,128)(2,1)}, u32[]{:S(2)}) copy-start(bf16[512,8,72]{0,2,1:T(8,128)(2,1)} %copy.40) | copy-start | bytes 1769476
  136.6 5.9 %copy-start.5 = (bf16[512,1,8,72]{0,3,2,1:T(8,128)(2,1)S(1)}, bf16[512,1,8,72]{0,3,2,1:T(8,128)(2,1)}, u32[]{:S(2)}) copy-start(bf16[512,1,8,72]{0,3,2,1:T(8,128)(2,1)} %copy.52) | copy-start | bytes 1769476
  207.3 31.8 %all-to-all-start.3 = ((bf16[32,2,13824]{2,1,0:T(2,128)(2,1)}), bf16[32,2,13824]{2,1,0:T(2,128)(2,1)}, u32[]{:S(2)}, u32[]{:S(2)}) async-start(bf16[32,2,13824]{2,1,0:T(2,128)(2,1)} %reshape.186), calls=%async_computation.3 | async-start | bytes 3538944 | tf_op jit(solution)/shard_map/all_to_all | solution.py:156
  216.6 299.3 %all-reduce.5.cloned.1.call-start = ((), (), s32[]{:S(2)}) async-start(), calls=%async_computation.4 | async-start | bytes 42467328
  290.3 3.0 copy-start.2
  293.3 6.1 %copy-start.3 = (bf16[1,16,16,1152]{3,2,1,0:T(8,128)(2,1)S(1)}, bf16[1,16,16,1152]{3,2,1,0:T(8,128)(2,1)}, u32[]{:S(2)}) copy-start(bf16[1,16,16,1152]{3,2,1,0:T(8,128)(2,1)} %param.13) | copy-start | bytes 1769476
Sparse Core Ops, SparseCore 0:
  290.4 225.4 all-reduce.4
where the time goes:
time: 535 us; the launch traced here: 526 us
  waiting for transfers between devices  239 us (45%)
  local copies, waits for them, and re-layouts  121 us (23%)
  matrix products  84.6 us (16%)
  starting transfers between devices  36.9 us (7%)
  other arithmetic  29.9 us (6%)
  between operations  14.4 us (3%)
    unnamed x2, waiting for transfers between devices  215 us
    unnamed x27, local copies, waits for them, and re-layouts  37.1 us
    all_to_all x1, waiting for transfers between devices, on_device(): lax.all_to_all(split_items(projected, frames, 3, devices), 'seq', split_a...  20 us
    unnamed x2, other arithmetic  19.9 us
    dot_general x1, matrix products, one_block(): jnp.einsum('hqk,khd->qhd', score_grad, keys, preferred_element_type=jnp.f...  15.1 us
    reshape x4, local copies, waits for them, and re-layouts, split_items(): values.reshape(frames, local, groups, HG, inner).transpose(3, 0, 1, 2, 4)  14.8 us
    dot_general x1, matrix products, one_block(): jnp.einsum('hqk,qhd->khd', score_grad, query_block, preferred_element_typ...  14.5 us
    dot_general x2, matrix products, contract(): lax.dot_general(left, right, (((0,), (0,)), ((), ())), preferred_element_...  14.2 us
  transfers between devices with their start and end apart: 5, of which 3 were waited for; matrix products, arithmetic and copies ran while one was open for 24% of the time, Pallas kernels for 0%

commit v1 on v0

v1 whole, which is shorter than its diff:
```python
import functools
import math

import jax
import jax.numpy as jnp
from jax import lax
from jax.experimental import pallas as pl
from jax.experimental.pallas import tpu as pltpu
from jax.sharding import PartitionSpec as P

MESH = pl.DeviceIdType.MESH
F32 = jnp.float32
BF16 = jnp.bfloat16

D = 1152
HD = 72
HC = 8
HW = HC * HD
T = 512
PART = 768
EPS = 1e-06
SCALE = 1.0 / math.sqrt(HD)
LOG2E = math.log2(math.e)
VMEM_LIMIT = 56 * 1024 * 1024

VMEM_SPEC = pl.BlockSpec(memory_space=pltpu.VMEM)
ANY_SPEC = pl.BlockSpec(memory_space=pl.ANY)


def dot(a, b, ca=1, cb=0):
    return lax.dot_general(a, b, (((ca,), (cb,)), ((), ())), preferred_element_type=F32)


class Place:
    def __init__(self):
        self.dp = lax.axis_index("dp")
        self.seq = lax.axis_index("seq")
        self.z_lo = self.dp // 2
        self.core = self.dp % 2
        self.x = self.seq // 8
        self.z_hi = (self.seq // 4) % 2
        self.y = self.seq % 4
        self.z = self.z_hi * 2 + self.z_lo
        self.half = self.seq // 16
        self.frame = self.seq % 16

    def partner(self):
        return (self.z_lo * 2 + 1 - self.core, self.seq)

    def owner(self, j):
        return (self.z_lo * 2 + self.half, 16 * self.core + j)

    def owner_is_me(self, j):
        return jnp.logical_and(self.half == self.core, 16 * self.core + j == self.seq)

    def ring(self, axis, k):
        if axis == "x":
            p = (self.x + k) % 4
            return p, (self.dp, p * 8 + self.z_hi * 4 + self.y)
        if axis == "y":
            p = (self.y + k) % 4
            return p, (self.dp, self.x * 8 + self.z_hi * 4 + p)
        p = (self.z + k) % 4
        return p, ((p % 2) * 2 + self.core, self.x * 8 + (p // 2) * 4 + self.y)

    def at(self, axis):
        return {"x": self.x, "y": self.y, "z": self.z}[axis]


def remote(src, dst, send, recv, device):
    return pltpu.make_async_remote_copy(
        src_ref=src, dst_ref=dst, send_sem=send, recv_sem=recv, device_id=device, device_id_type=MESH
    )


def gather_kernel(lat, cot, mods, xs, cs, mods2, send, recv, fsend, msend, mrecv):
    me = Place()
    barrier = pltpu.get_barrier_semaphore()

    def greet(j, _):
        @pl.when(jnp.logical_not(me.owner_is_me(j)))
        def _():
            pl.semaphore_signal(barrier, inc=1, device_id=me.owner(j), device_id_type=MESH)

        return 0

    lax.fori_loop(0, 16, greet, 0)
    pl.semaphore_signal(barrier, inc=1, device_id=me.partner(), device_id_type=MESH)
    pl.semaphore_wait(barrier, 17 - jnp.where(me.half == me.core, 1, 0))

    mine = remote(mods, mods2.at[me.core], msend.at[0], mrecv.at[0], me.partner())
    mine.start()
    own = pltpu.make_async_copy(mods, mods2.at[me.core], msend.at[1])
    own.start()

    pairs = ((lat, xs), (cot, cs))
    for a, (src, dst) in enumerate(pairs):

        def put(j, _, a=a, src=src, dst=dst):
            @pl.when(me.owner_is_me(j))
            def _():
                pltpu.make_async_copy(src.at[j], dst.at[me.seq], recv.at[a, me.seq]).start()

            @pl.when(jnp.logical_not(me.owner_is_me(j)))
            def _():
                remote(src.at[j], dst.at[me.seq], send.at[a, j], recv.at[a, me.seq], me.owner(j)).start()

            return 0

        lax.fori_loop(0, 16, put, 0)

    for a, (src, dst) in enumerate(pairs):

        def forward(j, _, a=a, src=src, dst=dst):
            s = 16 * me.core + j

            @pl.when(me.owner_is_me(j))
            def _():
                pltpu.make_async_copy(src.at[j], dst.at[s], recv.at[a, s]).wait()

            @pl.when(jnp.logical_not(me.owner_is_me(j)))
            def _():
                remote(src.at[j], dst.at[s], send.at[a, j], recv.at[a, s], me.owner(j)).wait_recv()

            remote(dst.at[s], dst.at[s], fsend.at[a, j], recv.at[a, s], me.partner()).start()
            return 0

        lax.fori_loop(0, 16, forward, 0)

    for a, (src, dst) in enumerate(pairs):

        def finish(j, _, a=a, src=src, dst=dst):
            s = 16 * me.core + j
            o = 16 * (1 - me.core) + j
            remote(dst.at[s], dst.at[o], fsend.at[a, j], recv.at[a, o], me.partner()).wait_recv()
            remote(dst.at[s], dst.at[s], fsend.at[a, j], recv.at[a, s], me.partner()).wait_send()

            @pl.when(jnp.logical_not(me.owner_is_me(j)))
            def _():
                remote(src.at[j], dst.at[me.seq], send.at[a, j], recv.at[a, me.seq], me.owner(j)).wait_send()

            return 0

        lax.fori_loop(0, 16, finish, 0)
    mine.wait_send()
    remote(mods, mods2.at[1 - me.core], msend.at[0], mrecv.at[0], me.partner()).wait_recv()
    own.wait()


def gather_tokens(lat, cot, mods):
    tokens = jax.ShapeDtypeStruct((32, 16, D), BF16)
    return pl.pallas_call(
        gather_kernel,
        out_shape=(tokens, tokens, jax.ShapeDtypeStruct((2, 16, D), BF16)),
        in_specs=[ANY_SPEC] * 3,
        out_specs=(ANY_SPEC,) * 3,
        scratch_shapes=[
            pltpu.SemaphoreType.DMA((2, 16)),
            pltpu.SemaphoreType.DMA((2, 32)),
            pltpu.SemaphoreType.DMA((2, 16)),
            pltpu.SemaphoreType.DMA((2,)),
            pltpu.SemaphoreType.DMA((1,)),
        ],
        compiler_params=pltpu.CompilerParams(collective_id=0, has_side_effects=True),
    )(lat, cot, mods)


def norm_block(values):
    floats = values.astype(F32)
    shifted = floats - jnp.mean(floats, -1, keepdims=True)
    variance = jnp.mean(shifted * shifted, -1, keepdims=True)
    inverse = lax.rsqrt(variance + EPS)
    return shifted * inverse, inverse


def attend_kernel(x_ref, c_ref, mods_ref, wqkv_ref, wout_ref, m_ref, bg_ref, att_ref, pg_ref, mg_ref, head, grad):
    sel = lax.axis_index("seq") // 16
    mods = mods_ref[sel].astype(F32)
    shift = mods[0:1]
    lift = 1.0 + mods[1:2]
    gate = mods[2:3]
    rows = 128

    def project(i, _):
        at = pl.ds(pl.multiple_of(i * rows, rows), rows)
        normed, _ = norm_block(x_ref[at, :])
        modulated = (normed * lift + shift).astype(BF16)
        m_ref[at, :] = modulated
        branch = (gate * c_ref[at, :].astype(F32)).astype(BF16)
        bg_ref[at, :] = branch
        projected = dot(modulated, wqkv_ref[...]).astype(BF16)
        upstream = dot(branch, wout_ref[...], 1, 1).astype(BF16)
        for h in range(3 * HC):
            head[h, at, 0:HD] = projected[:, h * HD : (h + 1) * HD]
        for h in range(HC):
            head[3 * HC + h, at, 0:HD] = upstream[:, h * HD : (h + 1) * HD]
        return 0

    lax.fori_loop(0, T // rows, project, 0)

    cut = 256

    def one_head(h, _):
        keys = head[HC + h, :, 0:HD]
        values = head[2 * HC + h, :, 0:HD]
        key_grad = jnp.zeros((T, HD), F32)
        value_grad = jnp.zeros((T, HD), F32)
        for b in range(T // cut):
            at = pl.ds(b * cut, cut)
            query = head[h, at, 0:HD]
            up = head[3 * HC + h, at, 0:HD]
            scores = dot(keys, query, 1, 1)
            top = jnp.max(scores, 0, keepdims=True)
            weights = jnp.exp2((scores - top) * (SCALE * LOG2E))
            probs = weights * (1.0 / jnp.sum(weights, 0, keepdims=True))
            low = probs.astype(BF16)
            mixed = dot(values, low, 0, 0)
            grad[h, at, 0:HD] = mixed.T.astype(BF16)
            value_grad += dot(low, up)
            dprobs = dot(values, up, 1, 1)
            weighted = probs * dprobs
            total = jnp.sum(weighted, 0, keepdims=True)
            score_grad = ((weighted - probs * total) * SCALE).astype(BF16)
            key_grad += dot(score_grad, query)
            grad[HC + h, at, 0:HD] = dot(keys, score_grad, 0, 0).T.astype(BF16)
        grad[2 * HC + h, :, 0:HD] = key_grad.astype(BF16)
        grad[3 * HC + h, :, 0:HD] = value_grad.astype(BF16)
        return 0

    lax.fori_loop(0, HC, one_head, 0)

    def merge(i, _):
        at = pl.ds(pl.multiple_of(i * rows, rows), rows)
        att_ref[at, :] = jnp.concatenate([grad[h, at, 0:HD] for h in range(HC)], 1)
        joined = jnp.concatenate([grad[HC + h, at, 0:HD] for h in range(3 * HC)], 1)
        pg_ref[at, :] = joined
        mg_ref[at, :] = dot(joined, wqkv_ref[...], 1, 1)
        return 0

    lax.fori_loop(0, T // rows, merge, 0)


def attend(x, c, mods2, wqkv, wout):
    return pl.pallas_call(
        attend_kernel,
        out_shape=(
            jax.ShapeDtypeStruct((T, D), BF16),
            jax.ShapeDtypeStruct((T, D), BF16),
            jax.ShapeDtypeStruct((T, HW), BF16),
            jax.ShapeDtypeStruct((T, 3 * HW), BF16),
            jax.ShapeDtypeStruct((T, D), F32),
        ),
        in_specs=[VMEM_SPEC] * 5,
        out_specs=(VMEM_SPEC,) * 5,
        scratch_shapes=[pltpu.VMEM((4 * HC, T, 128), BF16), pltpu.VMEM((4 * HC, T, 128), BF16)],
        compiler_params=pltpu.CompilerParams(vmem_limit_bytes=VMEM_LIMIT),
    )(x, c, mods2, wqkv, wout)


ORDERS = (("x", "y", "z"), ("y", "z", "x"), ("z", "x", "y"))


def natural_row(order, p):
    chunk = (p * 7282) >> 16
    inner = p - chunk * 9
    core = chunk & 1
    digits = {order[2]: (chunk >> 1) & 3, order[1]: (chunk >> 3) & 3, order[0]: chunk >> 5}
    z = digits["z"]
    block = (z & 1) * 64 + core * 32 + digits["x"] * 8 + (z >> 1) * 4 + digits["y"]
    return block * 9 + inner


def pick_rows(order, first, count):
    place = first + lax.broadcasted_iota(jnp.int32, (count, 1), 0)
    row = natural_row(order, place)
    column = lax.broadcasted_iota(jnp.int32, (count, D), 1)
    return jnp.where(row == column, 1.0, 0.0).astype(BF16)


def reduce_kernel(
    x_ref, c_ref, mods_ref, m_ref, bg_ref, att_ref, pg_ref, mg_ref, wout_ref,
    bo_ref, lg_ref, qkvg_ref, outg_ref,
    att_other, att_all, mg_other, bo_s, lg_s, bg_half, g1, r1, g2, r2, g3, r3, f4, r4,
    psend, precv, osend, orecv, s1, v1, s2, v2, s3, v3, s4, v4,
):
    me = Place()
    barrier = pltpu.get_barrier_semaphore()

    def greet(j, _):
        @pl.when(jnp.logical_not(me.owner_is_me(j)))
        def _():
            pl.semaphore_signal(barrier, inc=1, device_id=me.owner(j), device_id_type=MESH)

        return 0

    lax.fori_loop(0, 16, greet, 0)
    for axis in "xyz":
        for k in range(1, 4):
            pl.semaphore_signal(barrier, inc=1, device_id=me.ring(axis, k)[1], device_id_type=MESH)
    pl.semaphore_signal(barrier, inc=1, device_id=me.partner(), device_id_type=MESH)
    pl.semaphore_wait(barrier, 26 - jnp.where(me.half == me.core, 1, 0))

    other_rows = pl.ds(pl.multiple_of((1 - me.core) * 256, 256), 256)
    my_rows = pl.ds(pl.multiple_of(me.core * 256, 256), 256)
    swap_att = remote(att_ref, att_other, psend.at[0], precv.at[0], me.partner())
    swap_att.start()
    swap_mg = remote(mg_ref.at[other_rows], mg_other, psend.at[1], precv.at[1], me.partner())
    swap_mg.start()

    first = me.core == 0

    def ring_send(part, axis, k, src, dst, send, recv):
        p, device = me.ring(axis, k)
        return remote(src.at[part, p], dst.at[part, k - 1], send.at[part, k - 1], recv.at[part, k - 1], device)

    def products(part):
        order = ORDERS[part]
        for k in (1, 2, 3, 0):
            p, _ = me.ring(order[0], k)
            choose = pick_rows(order, p * 288, 288)
            left = dot(choose, m_ref[...], 1, 1).astype(BF16)
            if part < 2:
                block = dot(left, pg_ref[:, part * PART : (part + 1) * PART])
                g1[part, p] = block.astype(BF16)
            else:
                block = dot(left, pg_ref[:, 2 * PART : 3 * HW])
                a_left = dot(choose, att_all[...], 1, 1).astype(BF16)
                tail = dot(a_left, bg_half[...])
                g1[part, p] = jnp.concatenate([block, tail], 1).astype(BF16)
            if k > 0:
                ring_send(part, order[0], k, g1, r1, s1, v1).start()

    products(0)
    products(1)
    swap_att.wait()
    mine, theirs = att_ref[...], att_other[...]
    att_all[:, 0:HW] = jnp.where(first, mine, theirs)
    att_all[:, HW:] = jnp.where(first, theirs, mine)
    bg_half[...] = jnp.where(first, bg_ref[:, 0:HW], bg_ref[:, HW:])
    products(2)

    sel = me.half
    mods = mods_ref[sel].astype(F32)
    lift = 1.0 + mods[1:2]
    gate = mods[2:3]
    tokens = x_ref[my_rows, :]
    branch = dot(att_all[my_rows, :], wout_ref[...])
    out = (tokens.astype(F32) + gate * branch).astype(BF16)
    bo_s[...] = out.reshape(16, 16, D)

    def back(a, staged, out_ref):
        def put(j, _):
            @pl.when(me.owner_is_me(j))
            def _():
                pltpu.make_async_copy(staged.at[j], out_ref.at[me.frame], orecv.at[a, me.frame]).start()

            @pl.when(jnp.logical_not(me.owner_is_me(j)))
            def _():
                remote(staged.at[j], out_ref.at[me.frame], osend.at[a, j], orecv.at[a, me.frame], me.owner(j)).start()

            return 0

        lax.fori_loop(0, 16, put, 0)

    back(0, bo_s, bo_ref)
    swap_mg.wait()
    normed, inverse = norm_block(tokens)
    normed_grad = (mg_ref[my_rows, :] + mg_other[...]) * lift
    mean = jnp.mean(normed_grad, -1, keepdims=True)
    second = jnp.mean(normed_grad * normed, -1, keepdims=True)
    latent = c_ref[my_rows, :].astype(F32) + inverse * (normed_grad - mean - normed * second)
    lg_s[...] = latent.astype(BF16).reshape(16, 16, D)
    back(1, lg_s, lg_ref)

    for part in range(3):
        a, b, c = ORDERS[part]
        for k in range(1, 4):
            ring_send(part, a, k, g1, r1, s1, v1).wait_recv()
        total = g1[part, me.at(a)].astype(F32)
        for k in range(3):
            total += r1[part, k].astype(F32)
        for p in range(4):
            g2[part, p, 0:72] = total[p * 72 : (p + 1) * 72].astype(BF16)
            g2[part, p, 72:80] = jnp.zeros((8, PART), BF16)
        for k in range(1, 4):
            ring_send(part, b, k, g2, r2, s2, v2).start()
    for part in range(3):
        a, b, c = ORDERS[part]
        for k in range(1, 4):
            ring_send(part, b, k, g2, r2, s2, v2).wait_recv()
        total = g2[part, me.at(b)].astype(F32)
        for k in range(3):
            total += r2[part, k].astype(F32)
        for p in range(4):
            for core in range(2):
                at = p * 18 + core * 9
                g3[part, p, core * 16 : core * 16 + 16] = jnp.concatenate(
                    [total[at : at + 9], jnp.zeros((7, PART), F32)], 0
                ).astype(BF16)
        for k in range(1, 4):
            ring_send(part, c, k, g3, r3, s3, v3).start()
    for part in range(3):
        a, b, c = ORDERS[part]
        for k in range(1, 4):
            ring_send(part, c, k, g3, r3, s3, v3).wait_recv()
        total = g3[part, me.at(c)].astype(F32)
        for k in range(3):
            total += r3[part, k].astype(F32)
        f4[part] = total.reshape(2, 16, PART)
        remote(f4.at[part, 1 - me.core], r4.at[part], s4.at[part], v4.at[part], me.partner()).start()
    for part in range(3):
        remote(f4.at[part, 1 - me.core], r4.at[part], s4.at[part], v4.at[part], me.partner()).wait_recv()
    mine = jnp.concatenate([f4[part, me.core] for part in range(3)], 1)
    theirs = jnp.concatenate([r4[part] for part in range(3)], 1)
    low = jnp.where(first, mine, theirs)[0:9]
    high = jnp.where(first, theirs, mine)[0:9]
    for i in range(3):
        qkvg_ref[:, i * D : i * D + HW] = low[:, i * HW : (i + 1) * HW]
        qkvg_ref[:, i * D + HW : (i + 1) * D] = high[:, i * HW : (i + 1) * HW]
    outg_ref[:, 0:HW] = low[:, 3 * HW :]
    outg_ref[:, HW:] = high[:, 3 * HW :]

    for part in range(3):
        a, b, c = ORDERS[part]
        for k in range(1, 4):
            ring_send(part, a, k, g1, r1, s1, v1).wait_send()
            ring_send(part, b, k, g2, r2, s2, v2).wait_send()
            ring_send(part, c, k, g3, r3, s3, v3).wait_send()
        remote(f4.at[part, 1 - me.core], r4.at[part], s4.at[part], v4.at[part], me.partner()).wait_send()

    for a, (staged, out_ref) in enumerate(((bo_s, bo_ref), (lg_s, lg_ref))):

        def finish(j, _, a=a, staged=staged, out_ref=out_ref):
            @pl.when(me.owner_is_me(j))
            def _():
                pltpu.make_async_copy(staged.at[j], out_ref.at[j], orecv.at[a, j]).wait()

            @pl.when(jnp.logical_not(me.owner_is_me(j)))
            def _():
                copy = remote(staged.at[j], out_ref.at[j], osend.at[a, j], orecv.at[a, j], me.owner(j))
                copy.wait_recv()
                copy.wait_send()

            return 0

        lax.fori_loop(0, 16, finish, 0)


def reduce_all(*operands):
    dma = pltpu.SemaphoreType.DMA
    return pl.pallas_call(
        reduce_kernel,
        out_shape=(
            jax.ShapeDtypeStruct((16, 16, D), BF16),
            jax.ShapeDtypeStruct((16, 16, D), BF16),
            jax.ShapeDtypeStruct((9, 3 * D), F32),
            jax.ShapeDtypeStruct((9, D), F32),
        ),
        in_specs=[VMEM_SPEC] * 9,
        out_specs=(ANY_SPEC, ANY_SPEC, VMEM_SPEC, VMEM_SPEC),
        scratch_shapes=[
            pltpu.VMEM((T, HW), BF16),
            pltpu.VMEM((T, D), BF16),
            pltpu.VMEM((T // 2, D), F32),
            pltpu.VMEM((16, 16, D), BF16),
            pltpu.VMEM((16, 16, D), BF16),
            pltpu.VMEM((T, HW), BF16),
            pltpu.VMEM((3, 4, 288, PART), BF16),
            pltpu.VMEM((3, 3, 288, PART), BF16),
            pltpu.VMEM((3, 4, 80, PART), BF16),
            pltpu.VMEM((3, 3, 80, PART), BF16),
            pltpu.VMEM((3, 4, 32, PART), BF16),
            pltpu.VMEM((3, 3, 32, PART), BF16),
            pltpu.VMEM((3, 2, 16, PART), F32),
            pltpu.VMEM((3, 16, PART), F32),
            dma((2,)),
            dma((2,)),
            dma((2, 16)),
            dma((2, 16)),
            dma((3, 3)),
            dma((3, 3)),
            dma((3, 3)),
            dma((3, 3)),
            dma((3, 3)),
            dma((3, 3)),
            dma((3,)),
            dma((3,)),
        ],
        compiler_params=pltpu.CompilerParams(
            collective_id=1, has_side_effects=True, vmem_limit_bytes=VMEM_LIMIT
        ),
    )(*operands)


def on_device(latents, shift_mod, scale_mod, gate_mod, qkv_weight, out_weight, cotangent):
    core = lax.axis_index("dp") % 2
    mods = jnp.concatenate([shift_mod, scale_mod, gate_mod, jnp.zeros((13, D), BF16)], 0)
    wqkv = lax.dynamic_slice_in_dim(qkv_weight.reshape(D, 3, 2, HW), core, 1, 2).reshape(D, 3 * HW)
    wout = lax.dynamic_slice_in_dim(out_weight, core * HW, HW, 0)
    x, c, mods2 = gather_tokens(latents[0], cotangent[0], mods)
    x = x.reshape(T, D)
    c = c.reshape(T, D)
    m, bg, att, pg, mg = attend(x, c, mods2, wqkv, wout)
    bo, lg, qkvg, outg = reduce_all(x, c, mods2, m, bg, att, pg, mg, out_weight)
    return bo[None], lg[None], qkvg, outg


def solution(mesh):
    in_specs = (
        P("dp", None, "seq", None),
        P("dp", None),
        P("dp", None),
        P("dp", None),
        P(),
        P(),
        P("dp", None, "seq", None),
    )
    out_specs = (
        P("dp", None, "seq", None),
        P("dp", None, "seq", None),
        P(("dp", "seq"), None),
        P(("dp", "seq"), None),
    )
    return jax.shard_map(
        on_device, mesh=mesh, in_specs=in_specs, out_specs=out_specs, check_vma=False
    )
```

time: 535 us -> 164 us (0.31); the launches traced: 526 us -> 164 us
  waiting for transfers between devices: 239 us -> 0 us
  Pallas kernels: 0 us -> 132 us
  local copies, waits for them, and re-layouts: 121 us -> 30 us
  matrix products: 84.6 us -> 0 us
  starting transfers between devices: 36.9 us -> 0 us
  other arithmetic: 29.9 us -> 0.69 us
  between operations: 14.4 us -> 0.69 us
    unnamed x2 -> x0, waiting for transfers between devices: 215 us -> none
    pallas_call x0 -> x3, Pallas kernels: none -> 132 us  [the longest x1 72.2 us: reduce_all(): pl.pallas_call(reduce_kernel, out_shape=(jax.ShapeDtypeStruct((16, 16, D)...]
    dot_general x11 -> x0, matrix products: 77.3 us -> none  [the longest x1 15.1 us: one_block(): jnp.einsum('hqk,khd->qhd', score_grad, keys, preferred_element_type=jnp.f...]
    all_to_all x4 -> x0, starting transfers between devices: 36.8 us -> none  [the longest x1 11.3 us: on_device(): lax.all_to_all(split_items(attended_grad, frames, 1, devices), 'seq', spl...]
    reshape x9 -> x1, local copies, waits for them, and re-layouts: 41.5 us -> 6.58 us  [on_device(): lax.dynamic_slice_in_dim(qkv_weight.reshape(D, 3, 2, HW), core, 1, 2)]
    all_to_all x4 -> x0, waiting for transfers between devices: 24.2 us -> none  [the longest x1 20 us: on_device(): lax.all_to_all(split_items(projected, frames, 3, devices), 'seq', split_a...]
    unnamed x2 -> x0, other arithmetic: 19.9 us -> none
    unnamed x27 -> x15, local copies, waits for them, and re-layouts: 37.1 us -> 17.7 us
  transfers between devices with their start and end apart: 5 -> 0, of which waited for: 3 -> 0; matrix products, arithmetic and copies ran while one was open for 24% -> 0% of each run, Pallas kernels for 0% -> 0%
where the time goes in v1:
time: 164 us
  Pallas kernels  132 us (80%)
  local copies, waits for them, and re-layouts  30 us (18%)
    pallas_call x1, Pallas kernels, reduce_all(): pl.pallas_call(reduce_kernel, out_shape=(jax.ShapeDtypeStruct((16, 16, D)...  72.2 us
    pallas_call x1, Pallas kernels, attend(): pl.pallas_call(attend_kernel, out_shape=(jax.ShapeDtypeStruct((T, D), BF1...  32.7 us
    pallas_call x1, Pallas kernels, gather_tokens(): pl.pallas_call(gather_kernel, out_shape=(tokens, tokens, jax.ShapeDtypeSt...  27.3 us
    unnamed x15, local copies, waits for them, and re-layouts  17.7 us
    reshape x1, local copies, waits for them, and re-layouts, on_device(): lax.dynamic_slice_in_dim(qkv_weight.reshape(D, 3, 2, HW), core, 1, 2)  6.58 us
    dynamic_slice x1, local copies, waits for them, and re-layouts, on_device(): lax.dynamic_slice_in_dim(qkv_weight.reshape(D, 3, 2, HW), core, 1, 2)  4.4 us

profile of v1, /device:TPU:1, one launch (start us, length us, event | category | flops | bytes accessed | tf_op | source)
XLA Modules:
  0.0 163.7 jit_solution(15825087670080200928)
XLA Ops:
  0.6 11.5 %copy.12 = bf16[1152,3456]{0,1:T(8,128)(2,1)} copy(bf16[1152,3456]{1,0:T(8,128)(2,1)} %param.11) | data formatting | bytes 15925248 | tf_op args[4]
  12.2 4.4 %constant_dynamic-slice_fusion.1 = bf16[1152,3,1,576]{0,3,2,1:T(8,128)(2,1)} fusion(bf16[1152,3,2,576]{0,3,2,1:T(8,128)(2,1)} %bitcast.8, s32[]{:T(128)S(6)} %select_n.14), kind=kLoop, calls=%fused_computation.2 | loop fusion | bytes 7962628 | tf_op jit(solution)/shard_map/dynamic_slice | solution.py:498
  16.6 0.0 copy-start
  16.6 6.6 %copy.13.wqkv_ref = bf16[1152,1728]{1,0:T(8,128)(2,1)} copy(bf16[1152,1728]{0,1:T(8,128)(2,1)} %bitcast.9) | data formatting | bytes 7962624 | tf_op jit(solution)/shard_map/reshape | solution.py:498
  23.1 0.0 copy-start.2
  23.1 0.0 copy-start.3
  23.1 0.0 copy-start.4
  23.1 0.0 copy-done
  23.2 1.3 constant_dynamic-slice_fusion.wout_ref
  24.4 0.1 pad.3.clone
  24.5 0.0 copy-done.2
  24.5 0.0 copy-done.3
  24.5 0.0 copy-done.4
  24.5 0.7 maximum_maximum_fusion.mods
  25.2 27.3 %shard_map.102 = (bf16[32,16,1152]{2,1,0:T(8,128)(2,1)}, bf16[32,16,1152]{2,1,0:T(8,128)(2,1)}, bf16[2,16,1152]{2,1,0:T(8,128)(2,1)}) custom-call(bf16[16,16,1152]{2,1,0:T(8,128)(2,1)} %bitcast.14, bf16[16,16,1152]{2,1,0:T(8,128)(2,1)} %bitcast.15, bf16[16,1152]{1,0:T(8,128)(2,1)} %maximum_maximum_fusion.mods), custom_call_target="tpu_custom_call" | custom-call | tf_op jit(solution)/shard_map/pallas_call | solution.py:152
  52.5 32.7 %shard_map.103 = (bf16[512,1152]{1,0:T(8,128)(2,1)}, bf16[512,1152]{1,0:T(8,128)(2,1)}, bf16[512,576]{1,0:T(8,128)(2,1)}, bf16[512,1728]{1,0:T(8,128)(2,1)}, f32[512,1152]{1,0:T(8,128)}) custom-call(bf16[512,1152]{1,0:T(8,128)(2,1)} %bitcast.10, bf16[512,1152]{1,0:T(8,128)(2,1)} %bitcast.12, bf16[2,16,1152]{2,1,0:T(8,128)(2,1)} %get-tuple-element.18.mods_ref, ...), custom_call_target="tpu_custom_call" | custom-call | tf_op jit(solution)/shard_map/pallas_call | solution.py:244
  85.3 72.2 %shard_map.104 = (bf16[16,16,1152]{2,1,0:T(8,128)(2,1)}, bf16[16,16,1152]{2,1,0:T(8,128)(2,1)}, f32[9,3456]{1,0:T(8,128)}, f32[9,1152]{1,0:T(8,128)}) custom-call(bf16[512,1152]{1,0:T(8,128)(2,1)} %bitcast.11, bf16[512,1152]{1,0:T(8,128)(2,1)} %bitcast.13, bf16[2,16,1152]{2,1,0:T(8,128)(2,1)} %get-tuple-element.18.mods_ref, ...), custom_call_target="tpu_custom_call" | custom-call | tf_op jit(solution)/shard_map/pallas_call | solution.py:451
  157.5 0.0 copy-start.1
  157.5 2.0 %copy.18 = bf16[1,16,16,1152]{3,2,1,0:T(8,128)(2,1)} copy(bf16[1,16,16,1152]{3,2,1,0:T(8,128)(2,1)} %bitcast.17) | data formatting | bytes 1179648
  159.5 1.9 %copy.19 = bf16[1,16,16,1152]{3,2,1,0:T(8,128)(2,1)} copy(bf16[1,16,16,1152]{3,2,1,0:T(8,128)(2,1)} %bitcast.16) | data formatting | bytes 1179648
  161.4 1.6 copy.20
  163.1 0.0 copy-done.1
  163.1 0.6 copy.21
  (1 shorter events, 0.0 us)
Async XLA Ops:
  16.6 6.6 %copy-start = (bf16[1152,1152]{1,0:T(8,128)(2,1)S(1)}, bf16[1152,1152]{1,0:T(8,128)(2,1)}, u32[]{:S(2)}) copy-start(bf16[1152,1152]{1,0:T(8,128)(2,1)} %wout_ref.1) | copy-start | bytes 7962628
  23.1 1.4 copy-start.2
  23.1 1.4 copy-start.3
  23.1 1.4 copy-start.4
  157.5 5.5 %copy-start.1 = (f32[9,1152]{1,0:T(8,128)S(1)}, f32[9,1152]{1,0:T(8,128)}, u32[]{:S(2)}) copy-start(f32[9,1152]{1,0:T(8,128)} %get-tuple-element.35) | copy-start | bytes 124420

commit v2 on v1

v2 whole, which is shorter than its diff:
```python
import math

import jax
import jax.numpy as jnp
from jax import lax
from jax.experimental import pallas as pl
from jax.experimental.pallas import tpu as pltpu
from jax.sharding import PartitionSpec as P

MESH = pl.DeviceIdType.MESH
F32 = jnp.float32
BF16 = jnp.bfloat16

D = 1152
HD = 72
HC = 8
HW = HC * HD
T = 512
EPS = 1e-06
SCALE = 1.0 / math.sqrt(HD)
LOG2E = math.log2(math.e)
VMEM_LIMIT = 60 * 1024 * 1024
ROWS = 128
CUT = 256

ORDERS = (("x", "y", "z"), ("y", "z", "x"), ("z", "x", "y"))

VMEM_SPEC = pl.BlockSpec(memory_space=pltpu.VMEM)
ANY_SPEC = pl.BlockSpec(memory_space=pl.ANY)


def dot(a, b, ca=1, cb=0):
    return lax.dot_general(a, b, (((ca,), (cb,)), ((), ())), preferred_element_type=F32)


class Place:
    def __init__(self):
        self.dp = lax.axis_index("dp")
        self.seq = lax.axis_index("seq")
        self.z_lo = self.dp // 2
        self.core = self.dp % 2
        self.x = self.seq // 8
        self.z_hi = (self.seq // 4) % 2
        self.y = self.seq % 4
        self.z = self.z_hi * 2 + self.z_lo
        self.half = self.seq // 16
        self.frame = self.seq % 16

    def partner(self):
        return (self.z_lo * 2 + 1 - self.core, self.seq)

    def owner(self, j):
        return (self.z_lo * 2 + self.half, 16 * self.core + j)

    def owner_is_me(self, j):
        return jnp.logical_and(self.half == self.core, 16 * self.core + j == self.seq)

    def ring(self, axis, k):
        if axis == "x":
            p = (self.x + k) % 4
            return p, (self.dp, p * 8 + self.z_hi * 4 + self.y)
        if axis == "y":
            p = (self.y + k) % 4
            return p, (self.dp, self.x * 8 + self.z_hi * 4 + p)
        p = (self.z + k) % 4
        return p, ((p % 2) * 2 + self.core, self.x * 8 + (p // 2) * 4 + self.y)

    def at(self, axis):
        return {"x": self.x, "y": self.y, "z": self.z}[axis]


def remote(src, dst, send, recv, device):
    return pltpu.make_async_remote_copy(
        src_ref=src, dst_ref=dst, send_sem=send, recv_sem=recv, device_id=device, device_id_type=MESH
    )


def norm_block(values):
    floats = values.astype(F32)
    shifted = floats - jnp.mean(floats, -1, keepdims=True)
    variance = jnp.mean(shifted * shifted, -1, keepdims=True)
    inverse = lax.rsqrt(variance + EPS)
    return shifted * inverse, inverse


def pick_rows(part):
    order = ORDERS[part]
    p = lax.broadcasted_iota(jnp.int32, (384, 1), 0)
    chunk = (p * 10923) >> 16
    inner = p - chunk * 6 + part * 6
    digits = {order[2]: chunk & 3, order[1]: (chunk >> 2) & 3, order[0]: chunk >> 4}
    z = digits["z"]
    core = jnp.where(inner >= 9, 1, 0)
    block = (z & 1) * 64 + core * 32 + digits["x"] * 8 + (z >> 1) * 4 + digits["y"]
    row = block * 9 + inner - core * 9
    column = lax.broadcasted_iota(jnp.int32, (384, D), 1)
    return jnp.where(row == column, 1.0, 0.0).astype(BF16)


def block_kernel(
    lat, cot, shift_ref, scale_ref, gate_ref, wqkv_hbm, wout_hbm,
    bo_ref, lg_ref, qkvg_ref, outg_ref,
    xs, cs, mods, wfull, wqkv, wout, pick, m, mt, bg, bg_half, head, probs_s, att, att_other, at_t, grad, pg,
    mg, mg_other, bo_s, lg_s, g1, r1, g2, r2, g3, r3, f4, r4,
    send, recv, fsend, msem, wsem, psend, precv, osend, orecv, s1, v1, s2, v2, s3, v3, s4, v4,
):
    me = Place()
    first = me.core == 0

    weights = [pltpu.make_async_copy(wout_hbm, wout, wsem.at[3])]
    for i in range(3):
        columns = pl.ds(pl.multiple_of(i * D + me.core * 512, 128), 640)
        weights.append(pltpu.make_async_copy(wqkv_hbm.at[:, columns], wfull.at[i], wsem.at[i]))
    for copy in weights:
        copy.start()

    barrier = pltpu.get_barrier_semaphore()

    def greet(j, _):
        @pl.when(jnp.logical_not(me.owner_is_me(j)))
        def _():
            pl.semaphore_signal(barrier, inc=1, device_id=me.owner(j), device_id_type=MESH)

        return 0

    lax.fori_loop(0, 16, greet, 0)
    for axis in "xyz":
        for k in range(1, 4):
            pl.semaphore_signal(barrier, inc=1, device_id=me.ring(axis, k)[1], device_id_type=MESH)
    pl.semaphore_signal(barrier, inc=1, device_id=me.partner(), device_id_type=MESH)
    mods[me.core, 0:1] = shift_ref[...].astype(F32)
    mods[me.core, 1:2] = 1.0 + scale_ref[...].astype(F32)
    mods[me.core, 2:3] = gate_ref[...].astype(F32)
    mods[me.core, 3:8] = jnp.zeros((5, D), F32)
    pl.semaphore_wait(barrier, 26 - jnp.where(me.half == me.core, 1, 0))

    pairs = ((lat, xs), (cot, cs))
    for a, (src, dst) in enumerate(pairs):

        def put(t, _, a=a, src=src, dst=dst):
            j = (t + me.seq) % 16

            @pl.when(me.owner_is_me(j))
            def _():
                pltpu.make_async_copy(src.at[j], dst.at[me.seq], recv.at[a, me.seq]).start()

            @pl.when(jnp.logical_not(me.owner_is_me(j)))
            def _():
                remote(src.at[j], dst.at[me.seq], send.at[a, j], recv.at[a, me.seq], me.owner(j)).start()

            return 0

        lax.fori_loop(0, 16, put, 0)
    swap_mods = remote(mods.at[me.core], mods.at[me.core], msem.at[0], msem.at[1], me.partner())
    swap_mods.start()

    for part in range(3):
        pick[part * 384 : (part + 1) * 384] = pick_rows(part)
    for copy in weights:
        copy.wait()

    @pl.when(first)
    def _():
        for i in range(3):
            wqkv[:, i * HW : (i + 1) * HW] = wfull[i, :, 0:HW]

    @pl.when(jnp.logical_not(first))
    def _():
        for i in range(3):
            wqkv[:, i * HW : (i + 1) * HW] = wfull[i, :, 64:640]

    def share(a):
        src, dst = pairs[a]

        def forward(t, _):
            j = (me.frame - t) % 16
            s = 16 * me.core + j

            @pl.when(me.owner_is_me(j))
            def _():
                pltpu.make_async_copy(src.at[j], dst.at[s], recv.at[a, s]).wait()

            @pl.when(jnp.logical_not(me.owner_is_me(j)))
            def _():
                remote(src.at[j], dst.at[s], send.at[a, j], recv.at[a, s], me.owner(j)).wait_recv()

            remote(dst.at[s], dst.at[s], fsend.at[a, j], recv.at[a, s], me.partner()).start()
            return 0

        lax.fori_loop(0, 16, forward, 0)

        def arrive(j, _):
            s = 16 * me.core + j
            o = 16 * (1 - me.core) + j
            remote(dst.at[s], dst.at[o], fsend.at[a, j], recv.at[a, o], me.partner()).wait_recv()
            return 0

        lax.fori_loop(0, 16, arrive, 0)

    share(0)
    remote(mods.at[me.core], mods.at[1 - me.core], msem.at[0], msem.at[1], me.partner()).wait_recv()
    shift = mods[me.half, 0:1]
    lift = mods[me.half, 1:2]
    gate = mods[me.half, 2:3]

    def project(i, _):
        at = pl.ds(pl.multiple_of(i * ROWS, ROWS), ROWS)
        normed, _ = norm_block(xs[pl.ds(i * (ROWS // 16), ROWS // 16)].reshape(ROWS, D))
        modulated = (normed * lift + shift).astype(BF16)
        m[at, :] = modulated
        projected = dot(modulated, wqkv[...]).astype(BF16)
        for h in range(3 * HC):
            head[h, at, 0:HD] = projected[:, h * HD : (h + 1) * HD]
        return 0

    lax.fori_loop(0, T // ROWS, project, 0)

    def turn(part, _):
        at = pl.ds(pl.multiple_of(part * 384, 384), 384)
        mt[at, :] = dot(pick[at, :], m[...], 1, 1).astype(BF16)
        return 0

    lax.fori_loop(0, 3, turn, 0)
    share(1)

    def upstream(i, _):
        at = pl.ds(pl.multiple_of(i * ROWS, ROWS), ROWS)
        cotangent = cs[pl.ds(i * (ROWS // 16), ROWS // 16)].reshape(ROWS, D).astype(F32)
        branch = (gate * cotangent).astype(BF16)
        bg[at, :] = branch
        my_wout = wout[pl.ds(pl.multiple_of(me.core * HW, HW), HW), :]
        up = dot(branch, my_wout, 1, 1).astype(BF16)
        for h in range(HC):
            head[3 * HC + h, at, 0:HD] = up[:, h * HD : (h + 1) * HD]
        return 0

    lax.fori_loop(0, T // ROWS, upstream, 0)

    def forward_head(h, _):
        keys = head[HC + h, :, 0:HD]
        values = head[2 * HC + h, :, 0:HD]
        value_grad = jnp.zeros((T, HD), F32)
        for b in range(T // CUT):
            at = pl.ds(b * CUT, CUT)
            scores = dot(keys, head[h, at, 0:HD], 1, 1)
            top = jnp.max(scores, 0, keepdims=True)
            weights = jnp.exp2((scores - top) * (SCALE * LOG2E))
            probs = weights * (1.0 / jnp.sum(weights, 0, keepdims=True))
            probs_s[h, b] = probs
            low = probs.astype(BF16)
            grad[3 * HC + h, at, 0:HD] = dot(values, low, 0, 0).T.astype(BF16)
            value_grad += dot(low, head[3 * HC + h, at, 0:HD])
        grad[2 * HC + h, :, 0:HD] = value_grad.astype(BF16)
        return 0

    lax.fori_loop(0, HC, forward_head, 0)

    def join(first_head, target, column):
        def rows(i, _):
            at = pl.ds(pl.multiple_of(i * ROWS, ROWS), ROWS)
            target[at, column : column + HW] = jnp.concatenate(
                [grad[first_head + h, at, 0:HD] for h in range(HC)], 1
            )
            return 0

        lax.fori_loop(0, T // ROWS, rows, 0)

    join(3 * HC, att, 0)
    swap_att = remote(att, att_other, psend.at[0], precv.at[0], me.partner())
    swap_att.start()
    join(2 * HC, pg, 2 * HW)

    def ring_copy(chunk, part, axis, k, src, dst, send, recv):
        p, device = me.ring(axis, k)
        return remote(
            src.at[chunk, part, p],
            dst.at[chunk, part, k - 1],
            send.at[chunk, part, k - 1],
            recv.at[chunk, part, k - 1],
            device,
        )

    def stage_one(chunk, part, block):
        for p in range(4):
            g1[chunk, part, p] = block[p * 96 : (p + 1) * 96]
        for k in (2, 1, 3):
            ring_copy(chunk, part, ORDERS[part][0], k, g1, r1, s1, v1).start()

    def stage_two(chunk):
        for part in range(3):
            a, b, _ = ORDERS[part]
            for k in range(1, 4):
                ring_copy(chunk, part, a, k, g1, r1, s1, v1).wait_recv()
            total = g1[chunk, part, me.at(a)].astype(F32)
            for k in range(3):
                total += r1[chunk, part, k].astype(F32)
            for p in range(4):
                g2[chunk, part, p] = jnp.concatenate(
                    [total[p * 24 : (p + 1) * 24], jnp.zeros((8, D), F32)], 0
                ).astype(BF16)
            for k in (2, 1, 3):
                ring_copy(chunk, part, b, k, g2, r2, s2, v2).start()

    def stage_three(chunk):
        for part in range(3):
            _, b, c = ORDERS[part]
            for k in range(1, 4):
                ring_copy(chunk, part, b, k, g2, r2, s2, v2).wait_recv()
            total = g2[chunk, part, me.at(b)].astype(F32)
            for k in range(3):
                total += r2[chunk, part, k].astype(F32)
            for p in range(4):
                g3[chunk, part, p] = jnp.concatenate(
                    [total[p * 6 : (p + 1) * 6], jnp.zeros((10, D), F32)], 0
                ).astype(BF16)
            for k in (2, 1, 3):
                ring_copy(chunk, part, c, k, g3, r3, s3, v3).start()

    def swap_rows(chunk):
        return remote(f4.at[chunk, 1 - me.core], r4.at[chunk], s4.at[chunk], v4.at[chunk], me.partner())

    def stage_four(chunk):
        rows = []
        for part in range(3):
            _, _, c = ORDERS[part]
            for k in range(1, 4):
                ring_copy(chunk, part, c, k, g3, r3, s3, v3).wait_recv()
            total = g3[chunk, part, me.at(c)].astype(F32)
            for k in range(3):
                total += r3[chunk, part, k].astype(F32)
            rows.append(total[0:6])
        rows = jnp.concatenate(rows, 0)
        pad = jnp.zeros((7, D), F32)
        f4[chunk, 0] = jnp.concatenate([rows[0:9], pad], 0)
        f4[chunk, 1] = jnp.concatenate([rows[9:18], pad], 0)
        swap_rows(chunk).start()

    def stage_five(chunk):
        swap_rows(chunk).wait_recv()
        mine, theirs = f4[chunk, me.core], r4[chunk]
        return jnp.where(first, mine, theirs)[0:9], jnp.where(first, theirs, mine)[0:9]

    swap_att.wait()
    att_all = m
    mine, theirs = att[...], att_other[...]
    att_all[:, 0:HW] = jnp.where(first, mine, theirs)
    att_all[:, HW:] = jnp.where(first, theirs, mine)
    bg_half[...] = jnp.where(first, bg[:, 0:HW], bg[:, HW:])
    for part in range(3):
        at = pl.ds(part * 384, 384)
        at_t[at, :] = dot(pick[at, :], att_all[...], 1, 1).astype(BF16)
        value_part = dot(mt[at, :], pg[:, 2 * HW :])
        out_part = dot(at_t[at, :], bg_half[...])
        stage_one(0, part, jnp.concatenate([value_part, out_part], 1).astype(BF16))

    def back(a, staged, out_ref):
        def put(t, _):
            j = (me.frame - t) % 16

            @pl.when(me.owner_is_me(j))
            def _():
                pltpu.make_async_copy(staged.at[j], out_ref.at[me.frame], orecv.at[a, me.frame]).start()

            @pl.when(jnp.logical_not(me.owner_is_me(j)))
            def _():
                remote(staged.at[j], out_ref.at[me.frame], osend.at[a, j], orecv.at[a, me.frame], me.owner(j)).start()

            return 0

        lax.fori_loop(0, 16, put, 0)

    def finish_block(i, _):
        at = pl.ds(pl.multiple_of(me.core * 256 + i * ROWS, ROWS), ROWS)
        tiles = pl.ds(me.core * 16 + i * (ROWS // 16), ROWS // 16)
        branch = dot(att_all[at, :], wout[...])
        out = (xs[tiles].reshape(ROWS, D).astype(F32) + gate * branch).astype(BF16)
        bo_s[pl.ds(i * (ROWS // 16), ROWS // 16)] = out.reshape(ROWS // 16, 16, D)
        return 0

    lax.fori_loop(0, 256 // ROWS, finish_block, 0)
    back(0, bo_s, bo_ref)

    def backward_head(h, _):
        keys = head[HC + h, :, 0:HD]
        values = head[2 * HC + h, :, 0:HD]
        key_grad = jnp.zeros((T, HD), F32)
        for b in range(T // CUT):
            at = pl.ds(b * CUT, CUT)
            query = head[h, at, 0:HD]
            dprobs = dot(values, head[3 * HC + h, at, 0:HD], 1, 1)
            probs = probs_s[h, b]
            weighted = probs * dprobs
            total = jnp.sum(weighted, 0, keepdims=True)
            score_grad = ((weighted - probs * total) * SCALE).astype(BF16)
            key_grad += dot(score_grad, query)
            grad[h, at, 0:HD] = dot(keys, score_grad, 0, 0).T.astype(BF16)
        grad[HC + h, :, 0:HD] = key_grad.astype(BF16)
        return 0

    lax.fori_loop(0, 4, backward_head, 0)
    stage_two(0)
    lax.fori_loop(4, 6, backward_head, 0)
    stage_three(0)
    lax.fori_loop(6, 8, backward_head, 0)
    stage_four(0)
    join(0, pg, 0)
    join(HC, pg, HW)

    for part in range(3):
        at = pl.ds(part * 384, 384)
        stage_one(1, part, dot(mt[at, :], pg[:, 0 : 2 * HW]).astype(BF16))

    def modulated_grad(i, _):
        at = pl.ds(pl.multiple_of((1 - me.core) * 256 + i * ROWS, ROWS), ROWS)
        mg[pl.ds(pl.multiple_of(i * ROWS, ROWS), ROWS), :] = dot(pg[at, :], wqkv[...], 1, 1)
        return 0

    lax.fori_loop(0, 256 // ROWS, modulated_grad, 0)
    swap_mg = remote(mg, mg_other, psend.at[1], precv.at[1], me.partner())
    swap_mg.start()
    own_grad = dot(pg[pl.ds(pl.multiple_of(me.core * 256, 256), 256), :], wqkv[...], 1, 1)
    swap_mg.wait()
    for i in range(256 // ROWS):
        tiles = pl.ds(me.core * 16 + i * (ROWS // 16), ROWS // 16)
        normed, inverse = norm_block(xs[tiles].reshape(ROWS, D))
        normed_grad = (own_grad[i * ROWS : (i + 1) * ROWS] + mg_other[i * ROWS : (i + 1) * ROWS, :]) * lift
        mean = jnp.mean(normed_grad, -1, keepdims=True)
        second = jnp.mean(normed_grad * normed, -1, keepdims=True)
        latent = cs[tiles].reshape(ROWS, D).astype(F32) + inverse * (normed_grad - mean - normed * second)
        lg_s[i * (ROWS // 16) : (i + 1) * (ROWS // 16)] = latent.astype(BF16).reshape(ROWS // 16, 16, D)
    back(1, lg_s, lg_ref)

    stage_two(1)
    low, high = stage_five(0)
    qkvg_ref[:, 2 * D : 2 * D + HW] = low[:, 0:HW]
    qkvg_ref[:, 2 * D + HW : 3 * D] = high[:, 0:HW]
    outg_ref[:, 0:HW] = low[:, HW:]
    outg_ref[:, HW:] = high[:, HW:]
    stage_three(1)
    stage_four(1)
    low, high = stage_five(1)
    for i in range(2):
        qkvg_ref[:, i * D : i * D + HW] = low[:, i * HW : (i + 1) * HW]
        qkvg_ref[:, i * D + HW : (i + 1) * D] = high[:, i * HW : (i + 1) * HW]

    for chunk in range(2):
        for part in range(3):
            a, b, c = ORDERS[part]
            for k in range(1, 4):
                ring_copy(chunk, part, a, k, g1, r1, s1, v1).wait_send()
                ring_copy(chunk, part, b, k, g2, r2, s2, v2).wait_send()
                ring_copy(chunk, part, c, k, g3, r3, s3, v3).wait_send()
        swap_rows(chunk).wait_send()
    swap_mods.wait_send()
    for a, (src, dst) in enumerate(pairs):

        def sent(j, _, a=a, src=src, dst=dst):
            s = 16 * me.core + j
            remote(dst.at[s], dst.at[s], fsend.at[a, j], recv.at[a, s], me.partner()).wait_send()

            @pl.when(jnp.logical_not(me.owner_is_me(j)))
            def _():
                remote(src.at[j], dst.at[me.seq], send.at[a, j], recv.at[a, me.seq], me.owner(j)).wait_send()

            return 0

        lax.fori_loop(0, 16, sent, 0)
    for a, (staged, out_ref) in enumerate(((bo_s, bo_ref), (lg_s, lg_ref))):

        def finish(j, _, a=a, staged=staged, out_ref=out_ref):
            @pl.when(me.owner_is_me(j))
            def _():
                pltpu.make_async_copy(staged.at[j], out_ref.at[j], orecv.at[a, j]).wait()

            @pl.when(jnp.logical_not(me.owner_is_me(j)))
            def _():
                copy = remote(staged.at[j], out_ref.at[j], osend.at[a, j], orecv.at[a, j], me.owner(j))
                copy.wait_recv()
                copy.wait_send()

            return 0

        lax.fori_loop(0, 16, finish, 0)


def run_block(*operands):
    dma = pltpu.SemaphoreType.DMA
    vmem = pltpu.VMEM
    return pl.pallas_call(
        block_kernel,
        out_shape=(
            jax.ShapeDtypeStruct((16, 16, D), BF16),
            jax.ShapeDtypeStruct((16, 16, D), BF16),
            jax.ShapeDtypeStruct((9, 3 * D), F32),
            jax.ShapeDtypeStruct((9, D), F32),
        ),
        in_specs=[ANY_SPEC, ANY_SPEC, VMEM_SPEC, VMEM_SPEC, VMEM_SPEC, ANY_SPEC, ANY_SPEC],
        out_specs=(ANY_SPEC, ANY_SPEC, VMEM_SPEC, VMEM_SPEC),
        scratch_shapes=[
            vmem((32, 16, D), BF16),
            vmem((32, 16, D), BF16),
            vmem((2, 8, D), F32),
            vmem((3, D, 640), BF16),
            vmem((D, 3 * HW), BF16),
            vmem((D, D), BF16),
            vmem((D, D), BF16),
            vmem((T, D), BF16),
            vmem((D, T), BF16),
            vmem((T, D), BF16),
            vmem((T, HW), BF16),
            vmem((4 * HC, T, 128), BF16),
            vmem((HC, T // CUT, T, CUT), F32),
            vmem((T, HW), BF16),
            vmem((T, HW), BF16),
            vmem((D, T), BF16),
            vmem((4 * HC, T, 128), BF16),
            vmem((T, 3 * HW), BF16),
            vmem((T // 2, D), F32),
            vmem((T // 2, D), F32),
            vmem((16, 16, D), BF16),
            vmem((16, 16, D), BF16),
            vmem((2, 3, 4, 96, D), BF16),
            vmem((2, 3, 3, 96, D), BF16),
            vmem((2, 3, 4, 32, D), BF16),
            vmem((2, 3, 3, 32, D), BF16),
            vmem((2, 3, 4, 16, D), BF16),
            vmem((2, 3, 3, 16, D), BF16),
            vmem((2, 2, 16, D), F32),
            vmem((2, 16, D), F32),
            dma((2, 16)),
            dma((2, 32)),
            dma((2, 16)),
            dma((2,)),
            dma((4,)),
            dma((2,)),
            dma((2,)),
            dma((2, 16)),
            dma((2, 16)),
            dma((2, 3, 3)),
            dma((2, 3, 3)),
            dma((2, 3, 3)),
            dma((2, 3, 3)),
            dma((2, 3, 3)),
            dma((2, 3, 3)),
            dma((2,)),
            dma((2,)),
        ],
        compiler_params=pltpu.CompilerParams(
            collective_id=0, has_side_effects=True, vmem_limit_bytes=VMEM_LIMIT
        ),
    )(*operands)


def on_device(latents, shift_mod, scale_mod, gate_mod, qkv_weight, out_weight, cotangent):
    bo, lg, qkvg, outg = run_block(
        latents[0], cotangent[0], shift_mod, scale_mod, gate_mod, qkv_weight, out_weight
    )
    return bo[None], lg[None], qkvg, outg


def solution(mesh):
    in_specs = (
        P("dp", None, "seq", None),
        P("dp", None),
        P("dp", None),
        P("dp", None),
        P(),
        P(),
        P("dp", None, "seq", None),
    )
    out_specs = (
        P("dp", None, "seq", None),
        P("dp", None, "seq", None),
        P(("dp", "seq"), None),
        P(("dp", "seq"), None),
    )
    return jax.shard_map(
        on_device, mesh=mesh, in_specs=in_specs, out_specs=out_specs, check_vma=False
    )
```

time: 164 us -> 123 us (0.75)
  local copies, waits for them, and re-layouts: 30 us -> 7 us
  Pallas kernels: 132 us -> 115 us
    pallas_call x3 -> x1, Pallas kernels: 132 us -> 115 us  [run_block(): pl.pallas_call(block_kernel, out_shape=(jax.ShapeDtypeStruct((16, 16, D),...]
    unnamed x15 -> x4, local copies, waits for them, and re-layouts: 17.7 us -> 7 us
    reshape x1 -> x0, local copies, waits for them, and re-layouts: 6.58 us -> none  [on_device(): lax.dynamic_slice_in_dim(qkv_weight.reshape(D, 3, 2, HW), core, 1, 2)]
    dynamic_slice x2 -> x0, local copies, waits for them, and re-layouts: 5.67 us -> none  [the longest x1 4.4 us: on_device(): lax.dynamic_slice_in_dim(qkv_weight.reshape(D, 3, 2, HW), core, 1, 2)]
where the time goes in v2:
time: 123 us; the launch traced here: 122 us
  Pallas kernels  115 us (93%)
  local copies, waits for them, and re-layouts  7 us (6%)
    pallas_call x1, Pallas kernels, run_block(): pl.pallas_call(block_kernel, out_shape=(jax.ShapeDtypeStruct((16, 16, D),...  115 us
    unnamed x4, local copies, waits for them, and re-layouts  7 us

profile of v2, /device:TPU:1, one launch (start us, length us, event | category | flops | bytes accessed | tf_op | source)
XLA Modules:
  0.0 122.2 jit_solution(7823034227317039709)
XLA Ops:
  0.6 114.6 %shard_map.102 = (bf16[16,16,1152]{2,1,0:T(8,128)(2,1)}, bf16[16,16,1152]{2,1,0:T(8,128)(2,1)}, f32[9,3456]{1,0:T(8,128)}, f32[9,1152]{1,0:T(8,128)}) custom-call(bf16[16,16,1152]{2,1,0:T(8,128)(2,1)} %bitcast.4, bf16[16,16,1152]{2,1,0:T(8,128)(2,1)} %bitcast.5, bf16[1,1152]{1,0:T(2,128)(2,1)} %shift_ref.1, bf16[1,1152]{1,0:T(2,128)(2,1)} %scale_ref.1, ...), custom_call_target="tpu_custom_call" | custom-call | tf_op jit(solution)/shard_map/pallas_call | solution.py:489
  115.2 1.9 %copy.15 = bf16[1,16,16,1152]{3,2,1,0:T(8,128)(2,1)} copy(bf16[1,16,16,1152]{3,2,1,0:T(8,128)(2,1)} %bitcast.7) | data formatting | bytes 1179648
  117.1 1.9 %copy.16 = bf16[1,16,16,1152]{3,2,1,0:T(8,128)(2,1)} copy(bf16[1,16,16,1152]{3,2,1,0:T(8,128)(2,1)} %bitcast.6) | data formatting | bytes 1179648
  119.1 1.6 %copy.17 = f32[9,3456]{1,0:T(8,128)} copy(f32[9,3456]{1,0:T(8,128)} %get-tuple-element.18) | data formatting | bytes 248832
  120.7 1.5 %copy.18 = f32[9,1152]{1,0:T(8,128)} copy(f32[9,1152]{1,0:T(8,128)} %get-tuple-element.19) | data formatting | bytes 82944
